TPU v7x, 32 devices: a whole 2x2x4 slice. The times are simulated.
32 devices in a mesh: group: 2 (over y), ctx: 8 (over z, core), head: 2 (over x).
Axes of the slice: x: 2, y: 2, z: 4, core: 2. Of those that a mesh axis runs over, the one named last changes fastest.
Arguments:
- queries: bfloat16 [2048, 4096], P(('group', 'ctx'), 'head'), parts along dimension 0, may hold values from -6 to 6
- keys: bfloat16 [2048, 512], P(('group', 'ctx'), 'head'), parts along dimension 0, may hold values from -6 to 6
- values: bfloat16 [2048, 512], P(('group', 'ctx'), 'head'), parts along dimension 0, may hold values from -6 to 6
- sinks: float32 [64], P('head'), may hold values from 0 to 4
- segments: int32 [2048], P('group'), parts along dimension 0, may hold values from 0 to 3, never falling along the last dimension, each value on 1 to 768 neighbouring positions
- hidden_in: bfloat16 [2048, 2880], P(('group', 'ctx')), parts along dimension 0, may hold values from -6 to 6
- routes: int32 [2048, 4], P(('group', 'ctx')), parts along dimension 0, may hold values from 0 to 7, all different within a row; in each aligned block of 64 rows (0 to 63, 64 to 127, ...) at most 48 rows name the same one
- w_out: bfloat16 [4096, 2880], P('head'), may hold values from -0.09375 to 0.09375
- norm_gain: float32 [2880], replicated, may hold values from 0.1 to 1.9
- router: bfloat16 [2880, 8], replicated, may hold values from -0.109375 to 0.109375
- w_gate_up: bfloat16 [8, 2, 2880, 2880], P('ctx', None, None, 'head'), may hold values from -0.109375 to 0.109375
- w_down: bfloat16 [8, 2880, 2880], P('ctx', 'head'), may hold values from -0.109375 to 0.109375
Outputs:
- layer_out: bfloat16 [2048, 2880], P(('group', 'ctx', 'head')), parts along dimension 0
There are 2 independent parts, one for each index of `group`. A program takes and returns all parts, laid end to end along the dimension named above; an argument that names none is the same for every part. Nothing has to cross between parts.
Inputs may be any that keep to these rules, and one draw needn't show every extreme that they name: `routes`: each row names 4 different experts; in each aligned block of 64 rows no expert is named by more than 48 rows, a bound that some block reaches. `segments`: requests fill consecutive positions in order; the longest has 768 positions.
All inputs are finite; a program needn't handle non-finite values.
Results may differ from a plain program's by a relative error of at most 0.015.
Values may be sent and summed in bfloat16 or wider, within the bound.
No kernel may reach another device: no remote copies, remote signals or barrier semaphores. Data moves between devices by JAX's collectives and lax.ppermute only.
A program may use at most 128 MiB of HBM per device.

v0:
```python
import jax
import jax.numpy as jnp
from jax import lax
from jax.sharding import PartitionSpec as P

HEAD_SIZE = 64


masked_value = -1e30


def fold_step(state_in, pieces, query_grid, tok_pos, tok_seg, segments):
    running_max, running_sum, weighted = state_in
    key_piece, value_piece = pieces
    row_count = key_piece.shape[0]
    kv_groups = query_grid.shape[1]
    key_grid = key_piece.reshape(row_count, kv_groups, -1)
    value_grid = value_piece.reshape(row_count, kv_groups, -1)
    scores = jnp.einsum(
        "tcgd,ncd->cgtn", query_grid, key_grid, preferred_element_type=jnp.float32
    ) * HEAD_SIZE ** (-0.5)
    key_pos = jnp.arange(row_count, dtype=jnp.int32)
    visible = (key_pos[None, :] <= tok_pos[:, None]) & (segments[None, :] == tok_seg[:, None])
    scores = jnp.where(visible, scores, masked_value)
    new_max = jnp.maximum(running_max, jnp.max(scores, axis=-1))
    weights = jnp.where(visible, jnp.exp(scores - new_max[..., None]), 0.0)
    rescale = jnp.exp(running_max - new_max)
    running_sum = running_sum * rescale + jnp.sum(weights, axis=-1)
    weighted = weighted * rescale[..., None] + jnp.einsum(
        "cgtn,ncd->cgtd",
        weights.astype(jnp.bfloat16),
        value_grid,
        preferred_element_type=jnp.float32,
    )
    return (new_max, running_sum, weighted)


def rms_norm(residual, norm_gain):
    widened = residual.astype(jnp.float32)
    scale_rows = lax.rsqrt(jnp.mean(widened * widened, axis=-1, keepdims=True) + 1e-05)
    return (widened * scale_rows * norm_gain).astype(jnp.bfloat16)


def gate_weights(normed, router, route_ids):
    logits = jnp.dot(normed, router, preferred_element_type=jnp.float32)
    onehot = (
        route_ids[:, :, None] == jnp.arange(router.shape[1], dtype=jnp.int32)[None, None, :]
    ).astype(jnp.float32)
    picked = jnp.sum(onehot * logits[:, None, :], axis=-1)
    return jax.nn.softmax(picked, axis=-1)


def slot_index(route_ids, experts, capacity):
    flat_ids = route_ids.reshape(-1)
    onehot = (flat_ids[:, None] == jnp.arange(experts, dtype=jnp.int32)[None, :]).astype(jnp.int32)
    before = jnp.cumsum(onehot, axis=0) - onehot
    position = jnp.sum(before * onehot, axis=1)
    return (flat_ids * capacity + position).reshape(route_ids.shape)


def placer_matrix(slot_ids, slot_count):
    match = slot_ids[None, :, :] == jnp.arange(slot_count, dtype=jnp.int32)[:, None, None]
    return jnp.sum(match.astype(jnp.float32), axis=-1).astype(jnp.bfloat16)


def expert_piece(token_rows, w_gate_up, w_down):
    gate_pre = jnp.dot(token_rows, w_gate_up[0, 0], preferred_element_type=jnp.float32)
    up_pre = jnp.dot(token_rows, w_gate_up[0, 1], preferred_element_type=jnp.float32)
    activation = (gate_pre * jax.nn.sigmoid(1.702 * gate_pre) * (up_pre + 1.0)).astype(jnp.bfloat16)
    return jnp.dot(activation, w_down[0], preferred_element_type=jnp.float32).astype(jnp.bfloat16)


def body(
    queries,
    keys,
    values,
    sinks,
    segments,
    hidden_in,
    routes,
    w_out,
    norm_gain,
    router,
    w_gate_up,
    w_down,
):
    n_ctx = lax.axis_size("ctx")
    n_head = lax.axis_size("head")
    tok_count = queries.shape[0]
    top_count = routes.shape[1]
    kv_groups = keys.shape[1] // HEAD_SIZE
    group_share = queries.shape[1] // (kv_groups * HEAD_SIZE)
    q_start = lax.axis_index("ctx") * tok_count
    tok_pos = q_start + jnp.arange(tok_count, dtype=jnp.int32)
    tok_seg = lax.dynamic_slice_in_dim(segments, q_start, tok_count, 0)
    query_grid = queries.reshape(tok_count, kv_groups, group_share, HEAD_SIZE)
    sink_grid = sinks.reshape(kv_groups, group_share, 1) * jnp.ones((1, 1, tok_count), jnp.float32)
    initial = (
        sink_grid,
        jnp.ones_like(sink_grid),
        jnp.zeros((kv_groups, group_share, tok_count, HEAD_SIZE), jnp.float32),
    )
    running_max, running_sum, weighted = fold_step(
        initial,
        (
            lax.all_gather(keys, "ctx", axis=0, tiled=True),
            lax.all_gather(values, "ctx", axis=0, tiled=True),
        ),
        query_grid,
        tok_pos,
        tok_seg,
        segments,
    )
    attended = (
        (weighted / running_sum[..., None])
        .transpose(2, 0, 1, 3)
        .reshape(tok_count, -1)
        .astype(jnp.bfloat16)
    )
    own_rows = tok_count // n_head
    row_start = lax.axis_index("head") * own_rows
    capacity = max(2, min(tok_count // n_head, 3 * tok_count * top_count // (2 * n_head * n_ctx)))
    head_sums = lax.psum_scatter(
        jnp.dot(attended, w_out, preferred_element_type=jnp.float32).astype(jnp.bfloat16),
        "head",
        scatter_dimension=0,
        tiled=True,
    ).astype(jnp.float32)
    own_hidden = lax.dynamic_slice_in_dim(hidden_in, row_start, own_rows, 0)
    residual = (own_hidden.astype(jnp.float32) + head_sums).astype(jnp.bfloat16)
    normed = rms_norm(residual, norm_gain)
    own_routes = lax.dynamic_slice_in_dim(routes, row_start, own_rows, 0)
    gates = gate_weights(normed, router, own_routes)
    slot_ids = slot_index(own_routes, n_ctx, capacity)
    placer = placer_matrix(slot_ids, n_ctx * capacity)
    outgoing = jnp.dot(placer, normed, preferred_element_type=jnp.float32).astype(jnp.bfloat16)
    arrived = lax.all_to_all(outgoing, "ctx", split_axis=0, concat_axis=0, tiled=True)
    pieces = expert_piece(
        lax.all_gather(arrived, "head", axis=0, tiled=True), w_gate_up, w_down
    ).astype(jnp.float32)
    summed = lax.psum_scatter(pieces.astype(jnp.bfloat16), "head", scatter_dimension=0, tiled=True)
    returned = lax.all_to_all(summed, "ctx", split_axis=0, concat_axis=0, tiled=True)
    match = (
        slot_ids[:, :, None] == jnp.arange(n_ctx * capacity, dtype=jnp.int32)[None, None, :]
    ).astype(jnp.float32)
    combiner = jnp.sum(gates[:, :, None] * match, axis=1)
    expert_mix = jnp.dot(combiner, returned.astype(jnp.float32), precision=lax.Precision.HIGHEST)
    return (residual.astype(jnp.float32) + expert_mix).astype(jnp.bfloat16)


def solution(mesh):
    placed = (
        P(("group", "ctx"), "head"),
        P(("group", "ctx"), "head"),
        P(("group", "ctx"), "head"),
        P("head"),
        P("group"),
        P(("group", "ctx"), None),
        P(("group", "ctx"), None),
        P("head", None),
        P(),
        P(),
        P("ctx", None, None, "head"),
        P("ctx", "head", None),
    )
    return jax.shard_map(
        body,
        mesh=mesh,
        in_specs=placed,
        out_specs=P(("group", "ctx", "head"), None),
        check_vma=False,
    )
```

profile of v0, /device:TPU:0, one launch (start us, length us, event | category | flops | bytes accessed | tf_op | source)
XLA Modules:
  0.0 375.8 jit_solution(13164324825547892621)
XLA Ops:
  6.5 16.9 %all_gather.9 = bf16[1024,256]{1,0:T(8,128)(2,1)S(1)} all-gather(bf16[128,256]{1,0:T(8,128)(2,1)} %param.13), channel_id=1, replica_groups=mesh['group'=2,'ctx'=8,'head'=2] {'ctx'}, dimensions={0}, use_global_device_ids=true | all-gather | bytes 589824 | tf_op jit(solution)/shard_map/all_gather | solution.py:106
  23.5 0.2 copy.52
  23.7 1.3 copy.53
  25.0 0.7 mul.88
  25.7 0.8 dynamic_slice.10
  26.5 0.9 fusion.33
  27.4 2.4 fusion
  29.8 0.1 broadcast_maximum_fusion
  29.9 4.3 %fusion.1 = f32[4,8,128]{2,1,0:T(8,128)S(1)} fusion(f32[4,1024,128,8]{2,1,3,0:T(8,128)S(1)} %get-tuple-element.10, f32[4,8,128]{2,1,0:T(8,128)S(1)} %broadcast_maximum_fusion, pred[128,1024]{0,1:T(8,128)(4,1)S(1)} %fusion.33), kind=kLoop, calls=%fused_computation.3 | loop fusion | flops 20967424 | bytes 16941056 | tf_op jit(solution)/shard_map/reduce_sum | solution.py:28
  34.2 1.3 copy-done.2
  35.5 0.1 multiply_bitcast_fusion
  35.6 14.7 %all_gather.10 = bf16[1024,256]{1,0:T(8,128)(2,1)S(1)} all-gather(bf16[128,256]{1,0:T(8,128)(2,1)S(1)} %copy-done.3), channel_id=1, replica_groups=mesh['group'=2,'ctx'=8,'head'=2] {'ctx'}, dimensions={0}, use_global_device_ids=true | all-gather | bytes 589824 | tf_op jit(solution)/shard_map/all_gather | solution.py:107
  50.3 0.2 copy.54
  50.5 7.8 %divide_convert_fusion = bf16[128,4,8,64]{0,3,2,1:T(8,128)(2,1)S(1)} fusion(bf16[1024,4,64,1]{0,2,3,1:T(8,128)(2,1)S(1)} %bitcast.85, f32[4,1024,128,8]{2,1,3,0:T(8,128)} %copy-done.2, f32[4,8,128]{2,1,0:T(8,128)S(1)} %broadcast_maximum_fusion, pred[128,1024]{0,1:T(8,128)(4,1)S(1)} %fusion.33, f32[128,4,8]{0,2,1:T(8,128)S(1)} %get-tuple-element.8, ...), kind=kOutput, calls=%fused_computation.25 | convolution fusion | flops 558628864 | bytes 18006016 | tf_op jit(solution)/shard_map/cgtn,ncd->cgtd/dot_general | solution.py:29
  58.4 9.4 %convolution_convert_fusion.1 = bf16[128,2880]{1,0:T(8,128)(2,1)} fusion(bf16[128,2048]{0,1:T(8,128)(2,1)S(1)} %bitcast.84, bf16[2048,2880]{0,1:T(8,128)(2,1)} %param.19), kind=kOutput, calls=%fused_computation.18 | convolution fusion | flops 1510318080 | bytes 13058048 | tf_op jit(solution)/shard_map/dot_general | solution.py:124
  67.8 0.0 reduce-scatter.5.cloned.1.call-update
  67.9 0.2 all-gather.2.cloned.1.call-start
  68.1 0.1 constant_dynamic-slice_fusion
  68.2 0.1 copy.56
  68.3 0.1 eq.84
  68.4 0.1 eq.80
  68.5 0.3 constant_dynamic-slice_fusion.1
  68.8 0.3 copy.66
  69.1 0.6 reduce-window.6
  69.7 0.2 slice_reduce_fusion
  69.9 0.1 fusion.39
  70.0 0.1 reduce_sum.67
  70.2 0.1 copy.58
  70.2 0.1 multiply_add_fusion
  70.3 0.1 convert_reduce_fusion
  70.4 16.1 %reduce-scatter.5.cloned.1.call-done = bf16[64,2880]{1,0:T(8,128)(2,1)} async-done(((bf16[128,2880]{1,0:T(8,128)(2,1)}), bf16[64,2880]{1,0:T(8,128)(2,1)}) %reduce-scatter.5.cloned.1.call-update) | async-done | bytes 368656 | tf_op jit(solution)/shard_map/reduce_scatter | solution.py:123
  86.5 1.2 fusion.30
  87.8 2.3 convolution_convert_fusion
  90.0 2.9 copy.59
  93.0 57.1 %all_to_all.24 = bf16[8,48,2880]{2,1,0:T(8,128)(2,1)} all-to-all(bf16[8,48,2880]{2,1,0:T(8,128)(2,1)S(1)} %bitcast.80), channel_id=1, replica_groups=mesh['group'=2,'ctx'=8,'head'=2] {'ctx'}, dimensions={0} | all-to-all | bytes 4423680 | tf_op jit(solution)/shard_map/all_to_all | solution.py:137
  150.0 0.0 all-gather.2.cloned.1.call-update
  150.1 0.0 reduce-scatter.7.cloned.1.call-start
  150.1 58.5 %all-gather.2.cloned.1.call-done = bf16[768,2880]{1,0:T(8,128)(2,1)} async-done(((bf16[384,2880]{1,0:T(8,128)(2,1)}), bf16[768,2880]{1,0:T(8,128)(2,1)}) %all-gather.2.cloned.1.call-update) | async-done | bytes 4423696 | tf_op jit(solution)/shard_map/all_gather | solution.py:139
  208.6 12.3 %fusion.5 = f32[768,1440]{0,1:T(8,128)} fusion(bf16[768,2880]{1,0:T(8,128)(2,1)} %all-gather.2.cloned.1.call-done, bf16[1,2,2880,1440]{2,3,1,0:T(8,128)(2,1)} %param.22), kind=kOutput, calls=%fused_computation.7 | convolution fusion | flops 6370099200 | bytes 17424384 | tf_op jit(solution)/shard_map/dot_general | solution.py:68
  220.8 24.7 %fusion.14 = bf16[768,2880]{0,1:T(8,128)(2,1)} fusion(bf16[1,1440,2880]{2,1,0:T(8,128)(2,1)} %param.23, f32[768,1440]{0,1:T(8,128)} %fusion.5, bf16[768,2880]{1,0:T(8,128)(2,1)} %all-gather.2.cloned.1.call-done, bf16[1,2,2880,1440]{2,3,1,0:T(8,128)(2,1)} %param.22), kind=kOutput, calls=%fused_computation.15 | convolution fusion | flops 12751257600 | bytes 30326784 | tf_op jit(solution)/shard_map/dot_general | solution.py:70
  245.6 6.6 %copy.64 = bf16[768,2880]{1,0:T(8,128)(2,1)} copy(bf16[768,2880]{0,1:T(8,128)(2,1)} %fusion.14) | data formatting | bytes 8847360
  252.2 0.0 reduce-scatter.7.cloned.1.call-update
  252.2 58.0 %reduce-scatter.7.cloned.1.call-done = bf16[384,2880]{1,0:T(8,128)(2,1)} async-done(((bf16[768,2880]{1,0:T(8,128)(2,1)}), bf16[384,2880]{1,0:T(8,128)(2,1)}) %reduce-scatter.7.cloned.1.call-update) | async-done | bytes 2211856 | tf_op jit(solution)/shard_map/reduce_scatter | solution.py:141
  310.2 4.6 %all-to-all-start.1 = ((bf16[8,48,2880]{2,1,0:T(8,128)(2,1)}), bf16[8,48,2880]{2,1,0:T(8,128)(2,1)S(1)}, u32[]{:S(2)}, u32[]{:S(2)}) async-start(bf16[8,48,2880]{2,1,0:T(8,128)(2,1)} %bitcast.81), calls=%async_computation.2 | async-start | bytes 4521984 | tf_op jit(solution)/shard_map/all_to_all | solution.py:142
  314.8 0.3 fusion.35
  315.2 0.1 select_reduce_fusion
  315.3 52.0 %all-to-all-done.1 = bf16[8,48,2880]{2,1,0:T(8,128)(2,1)S(1)} async-done(((bf16[8,48,2880]{2,1,0:T(8,128)(2,1)}), bf16[8,48,2880]{2,1,0:T(8,128)(2,1)S(1)}, u32[]{:S(2)}, u32[]{:S(2)}) %all-to-all-start.1) | async-done | bytes 2211872 | tf_op jit(solution)/shard_map/all_to_all | solution.py:142
  367.4 1.8 fusion.19
  (23 shorter events, 0.2 us)
Async XLA Ops:
  6.5 62.0 %copy-start = (bf16[128,2880]{0,1:T(8,128)(2,1)S(1)}, bf16[128,2880]{0,1:T(8,128)(2,1)}, u32[]{:S(2)}) copy-start(bf16[128,2880]{0,1:T(8,128)(2,1)} %param.17) | copy-start | bytes 2211844
  6.5 80.0 %reduce-scatter.5.cloned.1.call-start = ((), (), s32[]{:S(2)}) async-start(), calls=%async_computation.4 | async-start | bytes 1130496 | tf_op jit(solution)/shard_map/reduce_scatter | solution.py:123
  29.8 5.7 %copy-start.2 = (f32[4,1024,128,8]{2,1,3,0:T(8,128)}, f32[4,1024,128,8]{2,1,3,0:T(8,128)S(1)}, u32[]{:S(2)}) copy-start(f32[4,1024,128,8]{2,1,3,0:T(8,128)S(1)} %get-tuple-element.10) | copy-start | bytes 50331652
  29.9 5.7 %copy-start.3 = (bf16[128,256]{1,0:T(8,128)(2,1)S(1)}, bf16[128,256]{1,0:T(8,128)(2,1)}, u32[]{:S(2)}) copy-start(bf16[128,256]{1,0:T(8,128)(2,1)} %param.14) | copy-start | bytes 196612
  58.4 9.7 %copy-start.5 = (s32[128,4]{0,1:T(4,128)S(1)}, s32[128,4]{0,1:T(4,128)}, u32[]{:S(2)}) copy-start(s32[128,4]{0,1:T(4,128)} %param.18) | copy-start | bytes 6148
  58.4 29.4 %copy-start.4 = (f32[2880]{0:T(1024)S(1)}, f32[2880]{0:T(1024)}, u32[]{:S(2)}) copy-start(f32[2880]{0:T(1024)} %param.20) | copy-start | bytes 34564
  67.9 140.7 %all-gather.2.cloned.1.call-start = ((), (), s32[]{:S(2)}) async-start(), calls=%async_computation.5 | async-start | bytes 6782976 | tf_op jit(solution)/shard_map/all_gather | solution.py:139
  150.1 160.1 %reduce-scatter.7.cloned.1.call-start = ((), (), s32[]{:S(2)}) async-start(), calls=%async_computation.6 | async-start | bytes 6782976 | tf_op jit(solution)/shard_map/reduce_scatter | solution.py:141
  245.6 69.2 %copy-start.6 = (bf16[2880,8]{0,1:T(8,128)(2,1)S(1)}, bf16[2880,8]{0,1:T(8,128)(2,1)}, u32[]{:S(2)}) copy-start(bf16[2880,8]{0,1:T(8,128)(2,1)} %param.21) | copy-start | bytes 138244
  245.6 123.7 %copy-start.1 = (bf16[128,2880]{0,1:T(8,128)(2,1)S(1)}, bf16[128,2880]{0,1:T(8,128)(2,1)}, u32[]{:S(2)}) copy-start(bf16[128,2880]{0,1:T(8,128)(2,1)} %param.17) | copy-start | bytes 2211844
  310.2 57.2 %all-to-all-start.1 = ((bf16[8,48,2880]{2,1,0:T(8,128)(2,1)}), bf16[8,48,2880]{2,1,0:T(8,128)(2,1)S(1)}, u32[]{:S(2)}, u32[]{:S(2)}) async-start(bf16[8,48,2880]{2,1,0:T(8,128)(2,1)} %bitcast.81), calls=%async_computation.2 | async-start | bytes 4521984 | tf_op jit(solution)/shard_map/all_to_all | solution.py:142
Sparse Core Ops, SparseCore 0:
  68.0 18.4 reduce-scatter.4
  150.2 58.3 all-gather.1
  252.3 57.8 reduce-scatter.6
where the time goes:
time: 376 us
  waiting for transfers between devices  185 us (49%)
  blocking collectives  88.7 us (24%)
  matrix products  61 us (16%)
  local copies, waits for them, and re-layouts  15.4 us (4%)
  between operations  13.3 us (4%)
  other arithmetic  7.75 us (2%)
  starting transfers between devices  4.86 us (1%)
    all_gather x1, waiting for transfers between devices, body(): lax.all_gather(arrived, 'head', axis=0, tiled=True)  58.5 us
    reduce_scatter x1, waiting for transfers between devices, body(): lax.psum_scatter(pieces.astype(jnp.bfloat16), 'head', scatter_dimension=0...  58 us
    all_to_all x1, blocking collectives, body(): lax.all_to_all(outgoing, 'ctx', split_axis=0, concat_axis=0, tiled=True)  57.1 us
    all_to_all x1, waiting for transfers between devices, body(): lax.all_to_all(summed, 'ctx', split_axis=0, concat_axis=0, tiled=True)  52 us
    dot_general x1, matrix products, expert_piece(): jnp.dot(activation, w_down[0], preferred_element_type=jnp.float32)  24.7 us
    all_gather x1, blocking collectives, body(): lax.all_gather(keys, 'ctx', axis=0, tiled=True)  16.9 us
    reduce_scatter x1, waiting for transfers between devices, body(): lax.psum_scatter(jnp.dot(attended, w_out, preferred_element_type=jnp.floa...  16.1 us
    all_gather x1, blocking collectives, body(): lax.all_gather(values, 'ctx', axis=0, tiled=True)  14.7 us
  transfers between devices with their start and end apart: 4, of which 4 were waited for; matrix products, arithmetic and copies ran while one was open for 1% of the time, Pallas kernels for 0%

commit v1 on v0

v1 whole, which is shorter than its diff:
```python
import functools

import jax
import jax.numpy as jnp
from jax import lax
from jax.experimental import pallas as pl
from jax.experimental.pallas import tpu as pltpu
from jax.sharding import PartitionSpec as P

HEAD_SIZE = 64
LANES = 128
CORES = 2
MIB = 1 << 20

masked_value = -1e30
NT = (((1,), (1,)), ((), ()))
NN = (((1,), (0,)), ((), ()))


def dot(a, b, dims):
    return lax.dot_general(a, b, dims, preferred_element_type=jnp.float32)


def attend_kernel(
    n_ctx, own_rows, place, q_ref, kv_own, kv_sib, sink_ref, tok_seg, segments, w_ref, *rest
):
    n_head = len(rest) - 6
    outs = rest[:n_head]
    weights, bias, attended, ordered, sums, arrived = rest[n_head:]
    tok_count = q_ref.shape[0]
    features = w_ref.shape[0]
    step = weights.shape[1]
    copies = []
    for i in range(0, features, step):
        rows = min(step, features - i)
        copies.append(
            pltpu.make_async_copy(
                w_ref.at[pl.ds(i, rows)],
                weights.at[i // step, pl.ds(0, rows)],
                arrived.at[i // step],
            )
        )
        copies[-1].start()
    ctx, head = place[0], place[1]
    half = kv_own.shape[0]
    kv_width = kv_own.shape[1] // 2
    kv_groups = kv_width // HEAD_SIZE
    share = q_ref.shape[1] // kv_width
    first = jnp.sum((segments[...] < tok_seg[...]).astype(jnp.float32), axis=1, keepdims=True)
    tok = ctx * tok_count + lax.broadcasted_iota(jnp.int32, (tok_count, half), 0)
    lane = lax.broadcasted_iota(jnp.int32, (tok_count, half), 1)
    hop = lane // tok_count
    z_here = ctx // CORES
    z_from = z_here - hop
    z_from = jnp.where(z_from < 0, z_from + n_ctx // CORES, z_from)
    core = ctx - z_here * CORES
    for i in range(2):
        owner = z_from * CORES + (core if i == 0 else 1 - core)
        pos = owner * tok_count + (lane - hop * tok_count)
        seen = (pos <= tok) & (pos.astype(jnp.float32) >= first)
        bias[i] = jnp.where(seen, 0.0, masked_value)
    for g in range(kv_groups):
        span = slice(g * HEAD_SIZE, (g + 1) * HEAD_SIZE)
        vspan = slice(kv_width + g * HEAD_SIZE, kv_width + (g + 1) * HEAD_SIZE)
        k0, k1 = kv_own[:, span], kv_sib[:, span]
        v0, v1 = kv_own[:, vspan], kv_sib[:, vspan]
        for j in range(share):
            h = g * share + j
            hs = slice(h * HEAD_SIZE, (h + 1) * HEAD_SIZE)
            q = q_ref[:, hs] * jnp.asarray(HEAD_SIZE**-0.5, q_ref.dtype)
            s0 = dot(q, k0, NT) + bias[0]
            s1 = dot(q, k1, NT) + bias[1]
            sink = sink_ref[h]
            top = jnp.maximum(
                jnp.maximum(
                    jnp.max(s0, axis=1, keepdims=True), jnp.max(s1, axis=1, keepdims=True)
                ),
                sink,
            )
            p0 = jnp.exp(s0 - top)
            p1 = jnp.exp(s1 - top)
            denom = (
                jnp.sum(p0, axis=1, keepdims=True)
                + jnp.sum(p1, axis=1, keepdims=True)
                + jnp.exp(sink - top)
            )
            o = dot(p0.astype(jnp.bfloat16), v0, NN) + dot(p1.astype(jnp.bfloat16), v1, NN)
            attended[:, hs] = (o / denom).astype(jnp.bfloat16)
    for j in range(n_head):
        source = lax.rem(head + n_head - j, n_head) * own_rows
        ordered[j * own_rows : (j + 1) * own_rows, :] = attended[
            pl.ds(pl.multiple_of(source, own_rows), own_rows), :
        ]
    for i in range(0, features, step):
        rows = min(step, features - i)
        copies[i // step].wait()
        sums[:, i : i + rows] = dot(ordered[...], weights[i // step, :rows, :], NT).astype(
            jnp.bfloat16
        )
    for j in range(n_head):
        outs[j][...] = sums[j * own_rows : (j + 1) * own_rows, :]


def attend(place, q, kv_own, kv_sib, sinks, tok_seg, segments, w_out_t, n_ctx, n_head):
    tok_count, columns = q.shape
    features = w_out_t.shape[0]
    own_rows = tok_count // n_head
    step = min(features, 5 * LANES)
    parts = -(-features // step)
    vmem = pl.BlockSpec(memory_space=pltpu.VMEM)
    smem = pl.BlockSpec(memory_space=pltpu.SMEM)
    n_keys = 2 * kv_own.shape[0]
    return pl.pallas_call(
        functools.partial(attend_kernel, n_ctx, own_rows),
        out_shape=[jax.ShapeDtypeStruct((own_rows, features), jnp.bfloat16)] * n_head,
        in_specs=[smem, vmem, vmem, vmem, smem, vmem, vmem, pl.BlockSpec(memory_space=pl.ANY)],
        out_specs=[vmem] * n_head,
        scratch_shapes=[
            pltpu.VMEM((parts, step, columns), jnp.bfloat16),
            pltpu.VMEM((2, tok_count, kv_own.shape[0]), jnp.float32),
            pltpu.VMEM((tok_count, columns), jnp.bfloat16),
            pltpu.VMEM((tok_count, columns), jnp.bfloat16),
            pltpu.VMEM((tok_count, features), jnp.bfloat16),
            pltpu.SemaphoreType.DMA((parts,)),
        ],
        compiler_params=pltpu.CompilerParams(vmem_limit_bytes=40 * MIB),
        cost_estimate=pl.CostEstimate(
            flops=4 * tok_count * columns * n_keys + 2 * tok_count * columns * features,
            bytes_accessed=2 * columns * features,
            transcendentals=tok_count * n_keys * columns // HEAD_SIZE,
        ),
        name="attend",
    )(place, q, kv_own, kv_sib, sinks, tok_seg, segments, w_out_t)


def norm_kernel(experts, hidden, routes, gain, router, *refs):
    sums, (residual_out, rows_out) = refs[:-2], refs[-2:]
    features = hidden.shape[1]
    total = sums[0][...].astype(jnp.float32)
    for other in sums[1:]:
        total = total + other[...].astype(jnp.float32)
    residual = (hidden[...].astype(jnp.float32) + total).astype(jnp.bfloat16)
    residual_out[...] = residual
    widened = residual.astype(jnp.float32)
    scale_rows = lax.rsqrt(jnp.mean(widened * widened, axis=-1, keepdims=True) + 1e-05)
    normed = (widened * scale_rows * gain[...]).astype(jnp.bfloat16)
    logits = dot(normed, router[...], NT)
    tail = rows_out.shape[1] - LANES
    offset = features - tail
    lane = lax.broadcasted_iota(jnp.int32, logits.shape, 1)
    expert = lane - offset
    expert = jnp.where(expert >= experts, expert - experts, expert)
    named = routes[:, 0:1] == expert
    for k in range(1, routes.shape[1]):
        named = named | (routes[:, k : k + 1] == expert)
    high_lanes = (lane >= offset) & (lane < offset + experts)
    low_lanes = (lane >= offset + experts) & (lane < offset + 2 * experts)
    chosen = jnp.where(named & (high_lanes | low_lanes), logits, masked_value)
    top = jnp.max(chosen, axis=1, keepdims=True)
    weight = jnp.exp(chosen - top)
    denom = jnp.sum(jnp.where(high_lanes, weight, 0.0), axis=1, keepdims=True)
    gates = weight / denom
    high = gates.astype(jnp.bfloat16).astype(jnp.float32)
    packed = jnp.where(high_lanes, high, jnp.where(low_lanes, gates - high, 0.0))
    rows_out[:, :features] = normed
    end = rows_out[:, tail:].astype(jnp.float32)
    rows_out[:, tail:] = jnp.where(lane < offset, end, packed).astype(jnp.bfloat16)


def norm_and_gates(sums, hidden, routes, gain, router_lanes, experts, width):
    rows, features = hidden.shape
    vmem = pl.BlockSpec(memory_space=pltpu.VMEM)
    return pl.pallas_call(
        functools.partial(norm_kernel, experts),
        out_shape=[
            jax.ShapeDtypeStruct((rows, features), jnp.bfloat16),
            jax.ShapeDtypeStruct((rows, width), jnp.bfloat16),
        ],
        in_specs=[vmem] * (4 + len(sums)),
        out_specs=[vmem] * 2,
        cost_estimate=pl.CostEstimate(
            flops=rows * features * LANES * 2,
            bytes_accessed=rows * features * 10,
            transcendentals=rows * LANES,
        ),
        name="norm_and_gates",
    )(hidden, routes, gain, router_lanes, *sums)


def expert_kernel(experts, place, near, far, gate_up, down, near_out, far_out, rows, total):
    i = pl.program_id(0)
    features = down.shape[1]
    count = near.shape[0]

    @pl.when(i == 0)
    def _():
        rows[:count, :] = near[:, :features]
        rows[count:, :] = far[:, :features]

    gate_pre = dot(rows[...], gate_up[0], NT)
    up_pre = dot(rows[...], gate_up[1], NT)
    act = (gate_pre * jax.nn.sigmoid(1.702 * gate_pre) * (up_pre + 1.0)).astype(jnp.bfloat16)
    part = dot(act, down[...], NN)

    @pl.when(i == 0)
    def _():
        total[...] = part

    @pl.when(i > 0)
    def _():
        total[...] += part

    @pl.when(i == pl.num_programs(0) - 1)
    def _():
        tail = near.shape[1] - LANES
        lane = lax.broadcasted_iota(jnp.int32, (count, LANES), 1) - (features - tail)
        mine = (lane == place[0]) | (lane == place[0] + experts)
        for ref, out, start in ((near, near_out, 0), (far, far_out, count)):
            packed = ref[:, tail:].astype(jnp.float32)
            gate = jnp.sum(jnp.where(mine, packed, 0.0), axis=1, keepdims=True)
            out[...] = (total[start : start + count, :] * gate).astype(jnp.bfloat16)


def block_of(hidden_units):
    for size in range(256, 15, -16):
        if hidden_units % size == 0:
            return size
    return hidden_units


def expert_rows(place, near, far, gate_up_t, down, experts):
    count, width = near.shape
    hidden_units, features = down.shape
    block = block_of(hidden_units)
    whole = lambda i: (0, 0)
    return pl.pallas_call(
        functools.partial(expert_kernel, experts),
        grid=(hidden_units // block,),
        out_shape=[jax.ShapeDtypeStruct((count, features), jnp.bfloat16)] * 2,
        in_specs=[
            pl.BlockSpec(memory_space=pltpu.SMEM),
            pl.BlockSpec((count, width), whole),
            pl.BlockSpec((count, width), whole),
            pl.BlockSpec((2, block, features), lambda i: (0, i, 0)),
            pl.BlockSpec((block, features), lambda i: (i, 0)),
        ],
        out_specs=[pl.BlockSpec((count, features), whole)] * 2,
        scratch_shapes=[
            pltpu.VMEM((2 * count, features), jnp.bfloat16),
            pltpu.VMEM((2 * count, features), jnp.float32),
        ],
        compiler_params=pltpu.CompilerParams(vmem_limit_bytes=40 * MIB),
        cost_estimate=pl.CostEstimate(
            flops=12 * count * hidden_units * features,
            bytes_accessed=6 * hidden_units * features,
            transcendentals=2 * count * hidden_units,
        ),
        name="expert_rows",
    )(place, near, far, gate_up_t, down)


def body(
    queries,
    keys,
    values,
    sinks,
    segments,
    hidden_in,
    routes,
    w_out,
    norm_gain,
    router,
    w_gate_up,
    w_down,
):
    n_ctx = lax.axis_size("ctx")
    n_head = lax.axis_size("head")
    n_z = n_ctx // CORES
    ctx = lax.axis_index("ctx")
    head = lax.axis_index("head")
    tok_count = queries.shape[0]
    features = hidden_in.shape[1]
    experts = router.shape[1]
    own_rows = tok_count // n_head
    width = -(-(features + 2 * experts) // LANES) * LANES

    to_sibling = [(i, i ^ 1) for i in range(n_ctx)]
    to_next_chip = [(i, (i + CORES) % n_ctx) for i in range(n_ctx)]

    def sibling(x):
        return lax.ppermute(x, "ctx", to_sibling)

    def next_chip(x):
        return lax.ppermute(x, "ctx", to_next_chip)

    def next_head(x, j):
        return lax.ppermute(x, "head", [(i, (i + j) % n_head) for i in range(n_head)])

    def add(*terms):
        total = terms[0].astype(jnp.float32)
        for term in terms[1:]:
            total = total + term.astype(jnp.float32)
        return total.astype(jnp.bfloat16)

    place = jnp.stack([ctx, head]).astype(jnp.int32)
    row_start = head * own_rows
    own_hidden = lax.dynamic_slice_in_dim(hidden_in, row_start, own_rows, 0)
    own_routes = lax.dynamic_slice_in_dim(routes, row_start, own_rows, 0)
    tok_seg = lax.dynamic_slice_in_dim(segments, ctx * tok_count, tok_count, 0)[:, None]
    tail = features - (width - LANES)
    router_lanes = jnp.pad(
        jnp.concatenate([router.T, router.T]), ((tail, LANES - tail - 2 * experts), (0, 0))
    )
    gate_up_t = jnp.swapaxes(w_gate_up[0], 1, 2)
    down = w_down[0]

    with jax.named_scope("keys_and_values"):
        kv = [jnp.concatenate([keys, values], axis=1)]
        for _ in range(n_z - 1):
            kv.append(next_chip(kv[-1]))
        kv_own = jnp.concatenate(kv)
        kv_sib = sibling(kv_own)

    with jax.named_scope("attention"):
        sums = attend(
            place, queries, kv_own, kv_sib, sinks, tok_seg, segments[None, :], w_out.T, n_ctx, n_head
        )

    with jax.named_scope("norm"):
        gathered = [sums[0]] + [next_head(sums[j], n_head - j) for j in range(1, n_head)]
        residual, rows = norm_and_gates(
            gathered, own_hidden, own_routes, norm_gain[None, :], router_lanes, experts, width
        )

    with jax.named_scope("rows_of_chips"):
        from_chip = [rows]
        for _ in range(n_z - 1):
            from_chip.append(next_chip(from_chip[-1]))

    arriving = None
    for hop in list(range(1, n_z)) + [0]:
        with jax.named_scope("experts"):
            near = jnp.concatenate(
                [from_chip[hop]] + [next_head(from_chip[hop], j) for j in range(1, n_head)]
            )
            far = sibling(near)
            near_out, far_out = expert_rows(place, near, far, gate_up_t, down, experts)
        with jax.named_scope("sum_back"):
            crossed = sibling(far_out)
            blocks = [
                (
                    near_out[j * own_rows : (j + 1) * own_rows],
                    crossed[j * own_rows : (j + 1) * own_rows],
                )
                for j in range(n_head)
            ]
            terms = list(blocks[0])
            for j in range(1, n_head):
                terms.append(next_head(add(*blocks[j]), n_head - j))
            if arriving is not None:
                terms.append(arriving)
            if hop != 0:
                arriving = next_chip(add(*terms))
    return add(residual, *terms)


def solution(mesh):
    placed = (
        P(("group", "ctx"), "head"),
        P(("group", "ctx"), "head"),
        P(("group", "ctx"), "head"),
        P("head"),
        P("group"),
        P(("group", "ctx"), None),
        P(("group", "ctx"), None),
        P("head", None),
        P(),
        P(),
        P("ctx", None, None, "head"),
        P("ctx", "head", None),
    )
    return jax.shard_map(
        body,
        mesh=mesh,
        in_specs=placed,
        out_specs=P(("group", "ctx", "head"), None),
        check_vma=False,
    )
```

time: 376 us -> 238 us (0.63)
  waiting for transfers between devices: 185 us -> 76.7 us
  blocking collectives: 88.7 us -> 0 us
  Pallas kernels: 0 us -> 73.7 us
  matrix products: 61 us -> 0 us
  local copies, waits for them, and re-layouts: 15.4 us -> 58.2 us
  between operations: 13.3 us -> 0.33 us
  starting transfers between devices: 4.86 us -> 14.4 us
  other arithmetic: 7.75 us -> 13.4 us
    ppermute x0 -> x27, waiting for transfers between devices: none -> 76.7 us  [the longest x9 51.9 us: next_chip(): return lax.ppermute(x, 'ctx', to_next_chip)]
    reduce_scatter x2 -> x0, waiting for transfers between devices: 74.1 us -> none  [the longest x1 58 us: body(): lax.psum_scatter(pieces.astype(jnp.bfloat16), 'head', scatter_dimension=0...]
    pallas_call x0 -> x6, Pallas kernels: none -> 73.7 us  [the longest x4 52 us: expert_rows(): pl.pallas_call(functools.partial(expert_kernel, experts), grid=(hidden_un...]
    dot_general x8 -> x0, matrix products: 61 us -> none  [the longest x1 24.7 us: expert_piece(): jnp.dot(activation, w_down[0], preferred_element_type=jnp.float32)]
    all_gather x1 -> x0, waiting for transfers between devices: 58.5 us -> none  [body(): lax.all_gather(arrived, 'head', axis=0, tiled=True)]
    all_to_all x1 -> x0, blocking collectives: 57.1 us -> none  [body(): lax.all_to_all(outgoing, 'ctx', split_axis=0, concat_axis=0, tiled=True)]
    all_to_all x1 -> x0, waiting for transfers between devices: 52 us -> none  [body(): lax.all_to_all(summed, 'ctx', split_axis=0, concat_axis=0, tiled=True)]
    all_gather x2 -> x0, blocking collectives: 31.6 us -> none  [the longest x1 16.9 us: body(): lax.all_gather(keys, 'ctx', axis=0, tiled=True)]
  transfers between devices with their start and end apart: 4 -> 27, of which waited for: 4 -> 13; matrix products, arithmetic and copies ran while one was open for 1% -> 18% of each run, Pallas kernels for 0% -> 22%
where the time goes in v1:
time: 238 us; the launch traced here: 237 us
  waiting for transfers between devices  76.7 us (32%)
  Pallas kernels  73.7 us (31%)
  local copies, waits for them, and re-layouts  58.2 us (24%)
  starting transfers between devices  14.4 us (6%)
  other arithmetic  13.4 us (6%)
    pallas_call x4, Pallas kernels, expert_rows(): pl.pallas_call(functools.partial(expert_kernel, experts), grid=(hidden_un...  52 us
    ppermute x9, waiting for transfers between devices, next_chip(): return lax.ppermute(x, 'ctx', to_next_chip)  51.9 us
    unnamed x67, local copies, waits for them, and re-layouts  37.8 us
    ppermute x9, waiting for transfers between devices, next_head(): lax.ppermute(x, 'head', [(i, (i + j) % n_head) for i in range(n_head)])  24.7 us
    pallas_call x1, Pallas kernels, attend(): pl.pallas_call(functools.partial(attend_kernel, n_ctx, own_rows), out_sha...  18.6 us
    convert_element_type x8, other arithmetic, add(): return total.astype(jnp.bfloat16)  12.3 us
    ppermute x9, starting transfers between devices, next_head(): lax.ppermute(x, 'head', [(i, (i + j) % n_head) for i in range(n_head)])  9.46 us
    slice x4, local copies, waits for them, and re-layouts, body(): crossed[j * own_rows:(j + 1) * own_rows]  8.74 us
  transfers between devices with their start and end apart: 27, of which 13 were waited for; matrix products, arithmetic and copies ran while one was open for 18% of the time, Pallas kernels for 22%

profile of v1, /device:TPU:0, one launch (start us, length us, event | category | flops | bytes accessed | tf_op | source)
XLA Modules:
  0.0 236.6 jit_solution(1809385940925046191)
XLA Ops:
  1.8 3.0 %collective-permute-start = (bf16[128,512]{1,0:T(8,128)(2,1)S(1)}, bf16[128,512]{1,0:T(8,128)(2,1)S(1)}, u32[]{:S(2)}, u32[]{:S(2)}) collective-permute-start(bf16[128,512]{1,0:T(8,128)(2,1)S(1)} %constant_dynamic-update-slice_fusion), channel_id=1, source_target_pairs={{0,4},{2,6},{4,8},{6,10},{8,12},{10,14},{12,0},{14,2},{1,5},{3,7},... | collective-permute-start | bytes 393224 | tf_op jit(solution)/shard_map/keys_and_values/ppermute | solution.py:294
  4.8 5.5 %collective-permute-done = bf16[128,512]{1,0:T(8,128)(2,1)S(1)} collective-permute-done((bf16[128,512]{1,0:T(8,128)(2,1)S(1)}, bf16[128,512]{1,0:T(8,128)(2,1)S(1)}, u32[]{:S(2)}, u32[]{:S(2)}) %collective-permute-start) | collective-permute-done | bytes 131104 | tf_op jit(solution)/shard_map/keys_and_values/ppermute | solution.py:294
  10.4 6.8 %collective-permute-done.1 = bf16[128,512]{1,0:T(8,128)(2,1)S(1)} collective-permute-done((bf16[128,512]{1,0:T(8,128)(2,1)S(1)}, bf16[128,512]{1,0:T(8,128)(2,1)S(1)}, u32[]{:S(2)}, u32[]{:S(2)}) %collective-permute-start.1) | collective-permute-done | bytes 131104 | tf_op jit(solution)/shard_map/keys_and_values/ppermute | solution.py:294
  17.1 6.8 %collective-permute-done.2 = bf16[128,512]{1,0:T(8,128)(2,1)S(1)} collective-permute-done((bf16[128,512]{1,0:T(8,128)(2,1)S(1)}, bf16[128,512]{1,0:T(8,128)(2,1)S(1)}, u32[]{:S(2)}, u32[]{:S(2)}) %collective-permute-start.2) | collective-permute-done | bytes 131104 | tf_op jit(solution)/shard_map/keys_and_values/ppermute | solution.py:294
  25.0 1.2 constant_dynamic-slice_fusion.1
  26.2 4.3 %copy-done.6 = bf16[2048,2880]{0,1:T(8,128)(2,1)S(1)} copy-done((bf16[2048,2880]{0,1:T(8,128)(2,1)S(1)}, bf16[2048,2880]{0,1:T(8,128)(2,1)}, u32[]{:S(2)}) %copy-start.6) | copy-done | bytes 11796504
  30.5 18.6 %attend.1 = (bf16[64,2880]{1,0:T(8,128)(2,1)S(1)}, bf16[64,2880]{1,0:T(8,128)(2,1)S(1)}) custom-call(s32[2]{0:T(128)S(1)} %pad_add_fusion.place, bf16[128,2048]{1,0:T(8,128)(2,1)S(1)} %copy-done.16, bf16[512,512]{1,0:T(8,128)(2,1)S(1)} %pad_maximum_fusion.kv_own, bf16[512,512]{1,0:T(8,128)(2,1)S(1)} %collective-permute-done.3.kv_sib, f32[32]{0:T(128)S(1)} %copy-done.19, ...), custom_call_target="tpu_custom_call" | custom-call | flops 2583691264 | bytes 11796480 | tf_op jit(solution)/shard_map/attention/attend/pallas_call | solution.py:113
  49.9 1.5 collective-permute-start.4
  54.7 6.3 %collective-permute-done.4.refs_1_ = bf16[64,2880]{1,0:T(8,128)(2,1)S(1)} collective-permute-done((bf16[64,2880]{1,0:T(8,128)(2,1)S(1)}, bf16[64,2880]{1,0:T(8,128)(2,1)S(1)}, u32[]{:S(2)}, u32[]{:S(2)}) %collective-permute-start.4) | collective-permute-done | bytes 368672 | tf_op jit(solution)/shard_map/norm/ppermute | solution.py:297
  61.8 3.0 %norm_and_gates.1 = (bf16[64,2880]{1,0:T(8,128)(2,1)}, bf16[64,2944]{1,0:T(8,128)(2,1)}) custom-call(bf16[64,2880]{1,0:T(8,128)(2,1)} %copy.31.hidden, s32[64,4]{1,0:T(8,128)} %copy.32.routes, f32[1,2880]{1,0:T(1,128)} %broadcast_in_dim.9.gain, bf16[128,2880]{1,0:T(8,128)(2,1)} %fusion.3.router, bf16[64,2880]{1,0:T(8,128)(2,1)} %copy-done.17, ...), custom_call_target="tpu_custom_call" | custom-call | flops 47185920 | bytes 1843200 | tf_op jit(solution)/shard_map/norm/norm_and_gates/pallas_call | solution.py:173
  64.8 1.5 collective-permute-start.5
  67.4 9.8 %collective-permute-done.9 = bf16[64,2944]{1,0:T(8,128)(2,1)S(1)} collective-permute-done((bf16[64,2944]{1,0:T(8,128)(2,1)}, bf16[64,2944]{1,0:T(8,128)(2,1)S(1)}, u32[]{:S(2)}, u32[]{:S(2)}) %collective-permute-start.9) | collective-permute-done | bytes 376864 | tf_op jit(solution)/shard_map/rows_of_chips/ppermute | solution.py:294
  77.2 1.5 collective-permute-start.20
  78.9 10.9 %collective-permute-done.10 = bf16[64,2944]{1,0:T(8,128)(2,1)S(1)} collective-permute-done((bf16[64,2944]{1,0:T(8,128)(2,1)S(1)}, bf16[64,2944]{1,0:T(8,128)(2,1)S(1)}, u32[]{:S(2)}, u32[]{:S(2)}) %collective-permute-start.10) | collective-permute-done | bytes 376864 | tf_op jit(solution)/shard_map/rows_of_chips/ppermute | solution.py:294
  90.4 7.6 %collective-permute-done.16 = bf16[64,2944]{1,0:T(8,128)(2,1)S(1)} collective-permute-done((bf16[64,2944]{1,0:T(8,128)(2,1)S(1)}, bf16[64,2944]{1,0:T(8,128)(2,1)S(1)}, u32[]{:S(2)}, u32[]{:S(2)}) %collective-permute-start.16) | collective-permute-done | bytes 376864 | tf_op jit(solution)/shard_map/experts/ppermute | solution.py:297
  98.2 3.4 %copy-done.2 = bf16[1,1440,2880]{2,1,0:T(8,128)(2,1)S(1)} copy-done((bf16[1,1440,2880]{2,1,0:T(8,128)(2,1)S(1)}, bf16[1,1440,2880]{2,1,0:T(8,128)(2,1)}, u32[]{:S(2)}) %copy-start.2) | copy-done | bytes 8294424
  101.6 13.0 %expert_rows.4 = (bf16[128,2880]{1,0:T(8,128)(2,1)S(1)}, bf16[128,2880]{1,0:T(8,128)(2,1)S(1)}) custom-call(s32[2]{0:T(128)S(1)} %pad_add_fusion.place, bf16[128,2944]{1,0:T(8,128)(2,1)S(1)} %constant_dynamic-update-slice_fusion.2.near, bf16[128,2944]{1,0:T(8,128)(2,1)S(1)} %collective-permute-done.6.far, bf16[2,1440,2880]{2,1,0:T(8,128)(2,1)} %bitcast.17, ...), custom_call_target="tpu_custom_call" | custom-call | flops 6370099200 | bytes 24883200 | tf_op jit(solution)/shard_map/experts/expert_rows/pallas_call | solution.py:236
  115.5 1.2 copy.19
  118.6 3.4 %copy-done.3 = bf16[1,1440,2880]{2,1,0:T(8,128)(2,1)S(1)} copy-done((bf16[1,1440,2880]{2,1,0:T(8,128)(2,1)S(1)}, bf16[1,1440,2880]{2,1,0:T(8,128)(2,1)}, u32[]{:S(2)}) %copy-start.3) | copy-done | bytes 8294424
  122.0 13.1 %expert_rows.7 = (bf16[128,2880]{1,0:T(8,128)(2,1)S(1)}, bf16[128,2880]{1,0:T(8,128)(2,1)S(1)}) custom-call(s32[2]{0:T(128)S(1)} %pad_add_fusion.place, bf16[128,2944]{1,0:T(8,128)(2,1)S(1)} %constant_dynamic-update-slice_fusion.8.near, bf16[128,2944]{1,0:T(8,128)(2,1)} %collective-permute-done.21.far, bf16[2,1440,2880]{2,1,0:T(8,128)(2,1)} %bitcast.18, ...), custom_call_target="tpu_custom_call" | custom-call | flops 6370099200 | bytes 24883200 | tf_op jit(solution)/shard_map/experts/expert_rows/pallas_call | solution.py:236
  136.9 2.2 copy.28
  139.7 3.4 %copy-done.4 = bf16[1,1440,2880]{2,1,0:T(8,128)(2,1)S(1)} copy-done((bf16[1,1440,2880]{2,1,0:T(8,128)(2,1)S(1)}, bf16[1,1440,2880]{2,1,0:T(8,128)(2,1)}, u32[]{:S(2)}) %copy-start.4) | copy-done | bytes 8294424
  143.1 13.0 %expert_rows.6 = (bf16[128,2880]{1,0:T(8,128)(2,1)S(1)}, bf16[128,2880]{1,0:T(8,128)(2,1)S(1)}) custom-call(s32[2]{0:T(128)S(1)} %pad_add_fusion.place, bf16[128,2944]{1,0:T(8,128)(2,1)S(1)} %constant_dynamic-update-slice_fusion.6.near, bf16[128,2944]{1,0:T(8,128)(2,1)S(1)} %collective-permute-done.17.far, bf16[2,1440,2880]{2,1,0:T(8,128)(2,1)} %bitcast.19, ...), custom_call_target="tpu_custom_call" | custom-call | flops 6370099200 | bytes 24883200 | tf_op jit(solution)/shard_map/experts/expert_rows/pallas_call | solution.py:236
  157.8 2.3 copy.25
  160.2 2.5 %fusion.7 = (bf16[64,2880]{0,1:T(8,128)(2,1)S(1)}, bf16[64,2880]{0,1:T(8,128)(2,1)}) fusion(bf16[128,2880]{0,1:T(8,128)(2,1)} %collective-permute-done.22), kind=kLoop, calls=%fused_computation.32 | loop fusion | bytes 1474560 | tf_op jit(solution)/shard_map/sum_back/slice | solution.py:353
  162.7 1.4 copy.40
  165.0 1.6 collective-permute-start.23
  166.9 3.4 %copy-done.5 = bf16[1,1440,2880]{2,1,0:T(8,128)(2,1)S(1)} copy-done((bf16[1,1440,2880]{2,1,0:T(8,128)(2,1)S(1)}, bf16[1,1440,2880]{2,1,0:T(8,128)(2,1)}, u32[]{:S(2)}) %copy-start.5) | copy-done | bytes 8294424
  170.3 13.0 %expert_rows.5 = (bf16[128,2880]{1,0:T(8,128)(2,1)S(1)}, bf16[128,2880]{1,0:T(8,128)(2,1)S(1)}) custom-call(s32[2]{0:T(128)S(1)} %pad_add_fusion.place, bf16[128,2944]{1,0:T(8,128)(2,1)S(1)} %constant_dynamic-update-slice_fusion.4.near, bf16[128,2944]{1,0:T(8,128)(2,1)S(1)} %collective-permute-done.13.far, bf16[2,1440,2880]{2,1,0:T(8,128)(2,1)} %bitcast.20, ...), custom_call_target="tpu_custom_call" | custom-call | flops 6370099200 | bytes 24883200 | tf_op jit(solution)/shard_map/experts/expert_rows/pallas_call | solution.py:236
  184.1 2.2 copy.22
  186.5 1.9 add_convert_fusion.3
  188.4 2.6 %fusion.6 = (bf16[64,2880]{0,1:T(8,128)(2,1)}, bf16[64,2880]{0,1:T(8,128)(2,1)S(1)}) fusion(bf16[128,2880]{0,1:T(8,128)(2,1)} %collective-permute-done.18), kind=kLoop, calls=%fused_computation.31 | loop fusion | bytes 1474560 | tf_op jit(solution)/shard_map/sum_back/slice | solution.py:353
  192.5 2.5 %fusion.4 = (bf16[64,2880]{0,1:T(8,128)(2,1)S(1)}, bf16[64,2880]{0,1:T(8,128)(2,1)}) fusion(bf16[128,2880]{0,1:T(8,128)(2,1)} %collective-permute-done.7), kind=kLoop, calls=%fused_computation.29 | loop fusion | bytes 1474560 | tf_op jit(solution)/shard_map/sum_back/slice | solution.py:353
  195.0 2.1 copy.34
  197.1 1.4 copy.37
  198.5 3.0 %collective-permute-done.24 = bf16[64,2880]{1,0:T(8,128)(2,1)} collective-permute-done((bf16[64,2880]{1,0:T(8,128)(2,1)}, bf16[64,2880]{1,0:T(8,128)(2,1)}, u32[]{:S(2)}, u32[]{:S(2)}) %collective-permute-start.24) | collective-permute-done | bytes 368672 | tf_op jit(solution)/shard_map/sum_back/ppermute | solution.py:294
  201.5 1.9 collective-permute-done.19
  203.5 2.0 add_convert_fusion.2
  205.5 1.1 fusion.5
  206.7 2.2 copy.36
  208.9 1.8 add_convert_fusion.6
  211.9 1.6 collective-permute-start.8
  213.9 4.0 %collective-permute-done.25 = bf16[64,2880]{1,0:T(8,128)(2,1)} collective-permute-done((bf16[64,2880]{1,0:T(8,128)(2,1)}, bf16[64,2880]{1,0:T(8,128)(2,1)}, u32[]{:S(2)}, u32[]{:S(2)}) %collective-permute-start.25) | collective-permute-done | bytes 368672 | tf_op jit(solution)/shard_map/sum_back/ppermute | solution.py:294
  217.8 4.9 %collective-permute-done.15 = bf16[64,2880]{1,0:T(8,128)(2,1)} collective-permute-done((bf16[64,2880]{1,0:T(8,128)(2,1)}, bf16[64,2880]{1,0:T(8,128)(2,1)}, u32[]{:S(2)}, u32[]{:S(2)}) %collective-permute-start.15) | collective-permute-done | bytes 368672 | tf_op jit(solution)/shard_map/sum_back/ppermute | solution.py:297
  222.7 2.0 add_convert_fusion.1
  225.4 3.9 %collective-permute-done.8 = bf16[64,2880]{1,0:T(8,128)(2,1)} collective-permute-done((bf16[64,2880]{1,0:T(8,128)(2,1)}, bf16[64,2880]{1,0:T(8,128)(2,1)}, u32[]{:S(2)}, u32[]{:S(2)}) %collective-permute-start.8) | collective-permute-done | bytes 368672 | tf_op jit(solution)/shard_map/sum_back/ppermute | solution.py:297
  229.3 5.3 %collective-permute-done.26 = bf16[64,2880]{1,0:T(8,128)(2,1)S(1)} collective-permute-done((bf16[64,2880]{1,0:T(8,128)(2,1)}, bf16[64,2880]{1,0:T(8,128)(2,1)S(1)}, u32[]{:S(2)}, u32[]{:S(2)}) %collective-permute-start.26) | collective-permute-done | bytes 368672 | tf_op jit(solution)/shard_map/sum_back/ppermute | solution.py:294
  234.5 2.1 add_convert_fusion
  (108 shorter events, 22.4 us)
Async XLA Ops:
  0.0 25.0 %copy-start = (bf16[128,2880]{0,1:T(8,128)(2,1)S(1)}, bf16[128,2880]{0,1:T(8,128)(2,1)}, u32[]{:S(2)}) copy-start(bf16[128,2880]{0,1:T(8,128)(2,1)} %param.17) | copy-start | bytes 2211844
  0.0 26.1 %copy-start.18 = (s32[1024]{0:T(1024)S(1)}, s32[1024]{0:T(1024)}, u32[]{:S(2)}) copy-start(s32[1024]{0:T(1024)} %param.16) | copy-start | bytes 12292
  0.0 26.1 %copy-start.16 = (bf16[128,2048]{1,0:T(8,128)(2,1)S(1)}, bf16[128,2048]{1,0:T(8,128)(2,1)}, u32[]{:S(2)}) copy-start(bf16[128,2048]{1,0:T(8,128)(2,1)} %q_ref.1) | copy-start | bytes 1572868
  0.0 26.1 %copy-start.19 = (f32[32]{0:T(128)S(1)}, f32[32]{0:T(128)}, u32[]{:S(2)}) copy-start(f32[32]{0:T(128)} %sink_ref.1) | copy-start | bytes 388
  1.8 8.5 %collective-permute-start = (bf16[128,512]{1,0:T(8,128)(2,1)S(1)}, bf16[128,512]{1,0:T(8,128)(2,1)S(1)}, u32[]{:S(2)}, u32[]{:S(2)}) collective-permute-start(bf16[128,512]{1,0:T(8,128)(2,1)S(1)} %constant_dynamic-update-slice_fusion), channel_id=1, source_target_pairs={{0,4},{2,6},{4,8},{6,10},{8,12},{10,14},{12,0},{14,2},{1,5},{3,7},... | collective-permute-start | bytes 393224 | tf_op jit(solution)/shard_map/keys_and_values/ppermute | solution.py:294
  10.4 6.8 %collective-permute-start.1 = (bf16[128,512]{1,0:T(8,128)(2,1)S(1)}, bf16[128,512]{1,0:T(8,128)(2,1)S(1)}, u32[]{:S(2)}, u32[]{:S(2)}) collective-permute-start(bf16[128,512]{1,0:T(8,128)(2,1)S(1)} %collective-permute-done), channel_id=1, source_target_pairs={{0,4},{2,6},{4,8},{6,10},{8,12},{10,14},{12,0},{14,2},{1,5},{3,7},... | collective-permute-start | bytes 393224 | tf_op jit(solution)/shard_map/keys_and_values/ppermute | solution.py:294
  17.1 6.8 %collective-permute-start.2 = (bf16[128,512]{1,0:T(8,128)(2,1)S(1)}, bf16[128,512]{1,0:T(8,128)(2,1)S(1)}, u32[]{:S(2)}, u32[]{:S(2)}) collective-permute-start(bf16[128,512]{1,0:T(8,128)(2,1)S(1)} %collective-permute-done.1), channel_id=1, source_target_pairs={{0,4},{2,6},{4,8},{6,10},{8,12},{10,14},{12,0},{14,2},{1,5},{3,7},... | collective-permute-start | bytes 393224 | tf_op jit(solution)/shard_map/keys_and_values/ppermute | solution.py:294
  23.9 2.2 collective-permute-start.3
  26.1 4.4 %copy-start.6 = (bf16[2048,2880]{0,1:T(8,128)(2,1)S(1)}, bf16[2048,2880]{0,1:T(8,128)(2,1)}, u32[]{:S(2)}) copy-start(bf16[2048,2880]{0,1:T(8,128)(2,1)} %param.19) | copy-start | bytes 35389444
  30.5 20.9 %copy-start.25 = (s32[128,4]{0,1:T(4,128)S(1)}, s32[128,4]{0,1:T(4,128)}, u32[]{:S(2)}) copy-start(s32[128,4]{0,1:T(4,128)} %param.18) | copy-start | bytes 6148
  30.5 21.0 %copy-start.20 = (bf16[64,2880]{0,1:T(8,128)(2,1)S(1)}, bf16[64,2880]{0,1:T(8,128)(2,1)}, u32[]{:S(2)}) copy-start(bf16[64,2880]{0,1:T(8,128)(2,1)} %constant_dynamic-slice_fusion.1) | copy-start | bytes 1105924
  30.5 22.7 %copy-start.24 = (f32[2880]{0:T(1024)S(1)}, f32[2880]{0:T(1024)}, u32[]{:S(2)}) copy-start(f32[2880]{0:T(1024)} %param.20) | copy-start | bytes 34564
  30.5 23.3 %copy-start.23 = (bf16[2880,8]{0,1:T(8,128)(2,1)S(1)}, bf16[2880,8]{0,1:T(8,128)(2,1)}, u32[]{:S(2)}) copy-start(bf16[2880,8]{0,1:T(8,128)(2,1)} %param.21) | copy-start | bytes 138244
  49.9 11.2 %collective-permute-start.4 = (bf16[64,2880]{1,0:T(8,128)(2,1)S(1)}, bf16[64,2880]{1,0:T(8,128)(2,1)S(1)}, u32[]{:S(2)}, u32[]{:S(2)}) collective-permute-start(bf16[64,2880]{1,0:T(8,128)(2,1)S(1)} %get-tuple-element.18), channel_id=1, source_target_pairs={{0,1},{1,0},{2,3},{3,2},{4,5},{5,4},{6,7},{7,6},{8,9},{9,8},{10,11... | collective-permute-start | bytes 1105928 | tf_op jit(solution)/shard_map/norm/ppermute | solution.py:297
  64.8 12.4 %collective-permute-start.9 = (bf16[64,2944]{1,0:T(8,128)(2,1)}, bf16[64,2944]{1,0:T(8,128)(2,1)S(1)}, u32[]{:S(2)}, u32[]{:S(2)}) collective-permute-start(bf16[64,2944]{1,0:T(8,128)(2,1)} %get-tuple-element.20), channel_id=1, source_target_pairs={{0,4},{2,6},{4,8},{6,10},{8,12},{10,14},{12,0},{14,2},{1,5},{3,7},... | collective-permute-start | bytes 1130504 | tf_op jit(solution)/shard_map/rows_of_chips/ppermute | solution.py:294
  64.8 13.9 %collective-permute-start.5 = (bf16[64,2944]{1,0:T(8,128)(2,1)}, bf16[64,2944]{1,0:T(8,128)(2,1)S(1)}, u32[]{:S(2)}, u32[]{:S(2)}) collective-permute-start(bf16[64,2944]{1,0:T(8,128)(2,1)} %get-tuple-element.20), channel_id=1, source_target_pairs={{0,1},{1,0},{2,3},{3,2},{4,5},{5,4},{6,7},{7,6},{8,9},{9,8},{10,11... | collective-permute-start | bytes 1130504 | tf_op jit(solution)/shard_map/experts/ppermute | solution.py:297
  77.2 13.0 %collective-permute-start.20 = (bf16[64,2944]{1,0:T(8,128)(2,1)S(1)}, bf16[64,2944]{1,0:T(8,128)(2,1)S(1)}, u32[]{:S(2)}, u32[]{:S(2)}) collective-permute-start(bf16[64,2944]{1,0:T(8,128)(2,1)S(1)} %collective-permute-done.9), channel_id=1, source_target_pairs={{0,1},{1,0},{2,3},{3,2},{4,5},{5,4},{6,7},{7,6},{8,9},{9,8},{10,11... | collective-permute-start | bytes 1130504 | tf_op jit(solution)/shard_map/experts/ppermute | solution.py:297
  78.7 11.0 %collective-permute-start.10 = (bf16[64,2944]{1,0:T(8,128)(2,1)S(1)}, bf16[64,2944]{1,0:T(8,128)(2,1)S(1)}, u32[]{:S(2)}, u32[]{:S(2)}) collective-permute-start(bf16[64,2944]{1,0:T(8,128)(2,1)S(1)} %collective-permute-done.9), channel_id=1, source_target_pairs={{0,4},{2,6},{4,8},{6,10},{8,12},{10,14},{12,0},{14,2},{1,5},{3,7},... | collective-permute-start | bytes 1130504 | tf_op jit(solution)/shard_map/rows_of_chips/ppermute | solution.py:294
  78.7 19.4 %collective-permute-start.6 = (bf16[128,2944]{1,0:T(8,128)(2,1)S(1)}, bf16[128,2944]{1,0:T(8,128)(2,1)S(1)}, u32[]{:S(2)}, u32[]{:S(2)}) collective-permute-start(bf16[128,2944]{1,0:T(8,128)(2,1)S(1)} %constant_dynamic-update-slice_fusion.2.near), channel_id=1, source_target_pairs={{0,2},{2,0},{4,6},{6,4},{8,10},{10,8},{12,14},{14,12},{1,3},{3,1},... | collective-permute-start | bytes 2261000 | tf_op jit(solution)/shard_map/experts/ppermute | solution.py:291
  89.7 8.3 %collective-permute-start.16 = (bf16[64,2944]{1,0:T(8,128)(2,1)S(1)}, bf16[64,2944]{1,0:T(8,128)(2,1)S(1)}, u32[]{:S(2)}, u32[]{:S(2)}) collective-permute-start(bf16[64,2944]{1,0:T(8,128)(2,1)S(1)} %collective-permute-done.10), channel_id=1, source_target_pairs={{0,1},{1,0},{2,3},{3,2},{4,5},{5,4},{6,7},{7,6},{8,9},{9,8},{10,11... | collective-permute-start | bytes 1130504 | tf_op jit(solution)/shard_map/experts/ppermute | solution.py:297
  90.2 28.3 %collective-permute-start.21 = (bf16[128,2944]{1,0:T(8,128)(2,1)S(1)}, bf16[128,2944]{1,0:T(8,128)(2,1)}, u32[]{:S(2)}, u32[]{:S(2)}) collective-permute-start(bf16[128,2944]{1,0:T(8,128)(2,1)S(1)} %constant_dynamic-update-slice_fusion.8.near), channel_id=1, source_target_pairs={{0,2},{2,0},{4,6},{6,4},{8,10},{10,8},{12,14},{14,12},{1,3},{3,1},... | collective-permute-start | bytes 2261000 | tf_op jit(solution)/shard_map/experts/ppermute | solution.py:291
  90.3 26.8 %collective-permute-start.11 = (bf16[64,2944]{1,0:T(8,128)(2,1)S(1)}, bf16[64,2944]{1,0:T(8,128)(2,1)}, u32[]{:S(2)}, u32[]{:S(2)}) collective-permute-start(bf16[64,2944]{1,0:T(8,128)(2,1)S(1)} %collective-permute-done.10), channel_id=1, source_target_pairs={{0,4},{2,6},{4,8},{6,10},{8,12},{10,14},{12,0},{14,2},{1,5},{3,7},... | collective-permute-start | bytes 1130504 | tf_op jit(solution)/shard_map/rows_of_chips/ppermute | solution.py:294
  98.1 41.6 %collective-permute-start.17 = (bf16[128,2944]{1,0:T(8,128)(2,1)S(1)}, bf16[128,2944]{1,0:T(8,128)(2,1)S(1)}, u32[]{:S(2)}, u32[]{:S(2)}) collective-permute-start(bf16[128,2944]{1,0:T(8,128)(2,1)S(1)} %constant_dynamic-update-slice_fusion.6.near), channel_id=1, source_target_pairs={{0,2},{2,0},{4,6},{6,4},{8,10},{10,8},{12,14},{14,12},{1,3},{3,1},... | collective-permute-start | bytes 2261000 | tf_op jit(solution)/shard_map/experts/ppermute | solution.py:291
  98.2 3.4 %copy-start.2 = (bf16[1,1440,2880]{2,1,0:T(8,128)(2,1)S(1)}, bf16[1,1440,2880]{2,1,0:T(8,128)(2,1)}, u32[]{:S(2)}) copy-start(bf16[1,1440,2880]{2,1,0:T(8,128)(2,1)} %param.23) | copy-start | bytes 24883204
  114.6 0.9 copy-start.14
  116.6 75.9 %collective-permute-start.7 = (bf16[128,2880]{0,1:T(8,128)(2,1)}, bf16[128,2880]{0,1:T(8,128)(2,1)}, u32[]{:S(2)}, u32[]{:S(2)}) collective-permute-start(bf16[128,2880]{0,1:T(8,128)(2,1)} %copy.19), channel_id=1, source_target_pairs={{0,2},{2,0},{4,6},{6,4},{8,10},{10,8},{12,14},{14,12},{1,3},{3,1},... | collective-permute-start | bytes 2211848 | tf_op jit(solution)/shard_map/sum_back/ppermute | solution.py:291
  117.1 22.0 %collective-permute-start.12 = (bf16[64,2944]{1,0:T(8,128)(2,1)}, bf16[64,2944]{1,0:T(8,128)(2,1)S(1)}, u32[]{:S(2)}, u32[]{:S(2)}) collective-permute-start(bf16[64,2944]{1,0:T(8,128)(2,1)} %collective-permute-done.11), channel_id=1, source_target_pairs={{0,1},{1,0},{2,3},{3,2},{4,5},{5,4},{6,7},{7,6},{8,9},{9,8},{10,11... | collective-permute-start | bytes 1130504 | tf_op jit(solution)/shard_map/experts/ppermute | solution.py:297
  118.6 3.4 %copy-start.3 = (bf16[1,1440,2880]{2,1,0:T(8,128)(2,1)S(1)}, bf16[1,1440,2880]{2,1,0:T(8,128)(2,1)}, u32[]{:S(2)}) copy-start(bf16[1,1440,2880]{2,1,0:T(8,128)(2,1)} %param.23) | copy-start | bytes 24883204
  135.1 0.9 copy-start.9
  139.1 21.1 %collective-permute-start.22 = (bf16[128,2880]{0,1:T(8,128)(2,1)}, bf16[128,2880]{0,1:T(8,128)(2,1)}, u32[]{:S(2)}, u32[]{:S(2)}) collective-permute-start(bf16[128,2880]{0,1:T(8,128)(2,1)} %copy.28), channel_id=1, source_target_pairs={{0,2},{2,0},{4,6},{6,4},{8,10},{10,8},{12,14},{14,12},{1,3},{3,1},... | collective-permute-start | bytes 2211848 | tf_op jit(solution)/shard_map/sum_back/ppermute | solution.py:291
  139.2 27.7 %collective-permute-start.13 = (bf16[128,2944]{1,0:T(8,128)(2,1)S(1)}, bf16[128,2944]{1,0:T(8,128)(2,1)S(1)}, u32[]{:S(2)}, u32[]{:S(2)}) collective-permute-start(bf16[128,2944]{1,0:T(8,128)(2,1)S(1)} %constant_dynamic-update-slice_fusion.4.near), channel_id=1, source_target_pairs={{0,2},{2,0},{4,6},{6,4},{8,10},{10,8},{12,14},{14,12},{1,3},{3,1},... | collective-permute-start | bytes 2261000 | tf_op jit(solution)/shard_map/experts/ppermute | solution.py:291
  139.7 3.4 %copy-start.4 = (bf16[1,1440,2880]{2,1,0:T(8,128)(2,1)S(1)}, bf16[1,1440,2880]{2,1,0:T(8,128)(2,1)}, u32[]{:S(2)}) copy-start(bf16[1,1440,2880]{2,1,0:T(8,128)(2,1)} %param.23) | copy-start | bytes 24883204
  157.0 0.9 copy-start.13
  160.2 4.0 %copy-start.10 = (bf16[128,2880]{1,0:T(8,128)(2,1)S(1)}, bf16[128,2880]{1,0:T(8,128)(2,1)}, u32[]{:S(2)}) copy-start(bf16[128,2880]{1,0:T(8,128)(2,1)} %copy-done.9) | copy-start | bytes 2211844
  160.2 28.3 %collective-permute-start.18 = (bf16[128,2880]{0,1:T(8,128)(2,1)}, bf16[128,2880]{0,1:T(8,128)(2,1)}, u32[]{:S(2)}, u32[]{:S(2)}) collective-permute-start(bf16[128,2880]{0,1:T(8,128)(2,1)} %copy.25), channel_id=1, source_target_pairs={{0,2},{2,0},{4,6},{6,4},{8,10},{10,8},{12,14},{14,12},{1,3},{3,1},... | collective-permute-start | bytes 2211848 | tf_op jit(solution)/shard_map/sum_back/ppermute | solution.py:291
  165.0 21.6 %collective-permute-start.23 = (bf16[64,2880]{1,0:T(8,128)(2,1)}, bf16[64,2880]{1,0:T(8,128)(2,1)}, u32[]{:S(2)}, u32[]{:S(2)}) collective-permute-start(bf16[64,2880]{1,0:T(8,128)(2,1)} %add_convert_fusion.4), channel_id=1, source_target_pairs={{0,1},{1,0},{2,3},{3,2},{4,5},{5,4},{6,7},{7,6},{8,9},{9,8},{10,11... | collective-permute-start | bytes 1105928 | tf_op jit(solution)/shard_map/sum_back/ppermute | solution.py:297
  166.9 3.4 %copy-start.5 = (bf16[1,1440,2880]{2,1,0:T(8,128)(2,1)S(1)}, bf16[1,1440,2880]{2,1,0:T(8,128)(2,1)}, u32[]{:S(2)}) copy-start(bf16[1,1440,2880]{2,1,0:T(8,128)(2,1)} %param.23) | copy-start | bytes 24883204
  186.4 19.1 %collective-permute-start.14 = (bf16[128,2880]{0,1:T(8,128)(2,1)}, bf16[128,2880]{0,1:T(8,128)(2,1)S(1)}, u32[]{:S(2)}, u32[]{:S(2)}) collective-permute-start(bf16[128,2880]{0,1:T(8,128)(2,1)} %copy.22), channel_id=1, source_target_pairs={{0,2},{2,0},{4,6},{6,4},{8,10},{10,8},{12,14},{14,12},{1,3},{3,1},... | collective-permute-start | bytes 2211848 | tf_op jit(solution)/shard_map/sum_back/ppermute | solution.py:291
  188.4 2.9 %copy-start.8 = (bf16[128,2880]{1,0:T(8,128)(2,1)S(1)}, bf16[128,2880]{1,0:T(8,128)(2,1)}, u32[]{:S(2)}) copy-start(bf16[128,2880]{1,0:T(8,128)(2,1)} %copy-done.7) | copy-start | bytes 2211844
  188.4 13.1 %collective-permute-start.24 = (bf16[64,2880]{1,0:T(8,128)(2,1)}, bf16[64,2880]{1,0:T(8,128)(2,1)}, u32[]{:S(2)}, u32[]{:S(2)}) collective-permute-start(bf16[64,2880]{1,0:T(8,128)(2,1)} %add_convert_fusion.3), channel_id=1, source_target_pairs={{0,4},{2,6},{4,8},{6,10},{8,12},{10,14},{12,0},{14,2},{1,5},{3,7},... | collective-permute-start | bytes 1105928 | tf_op jit(solution)/shard_map/sum_back/ppermute | solution.py:294
  192.1 11.3 %collective-permute-start.19 = (bf16[64,2880]{1,0:T(8,128)(2,1)}, bf16[64,2880]{1,0:T(8,128)(2,1)}, u32[]{:S(2)}, u32[]{:S(2)}) collective-permute-start(bf16[64,2880]{1,0:T(8,128)(2,1)} %add_convert_fusion.5), channel_id=1, source_target_pairs={{0,1},{1,0},{2,3},{3,2},{4,5},{5,4},{6,7},{7,6},{8,9},{9,8},{10,11... | collective-permute-start | bytes 1105928 | tf_op jit(solution)/shard_map/sum_back/ppermute | solution.py:297
  205.5 12.3 %collective-permute-start.25 = (bf16[64,2880]{1,0:T(8,128)(2,1)}, bf16[64,2880]{1,0:T(8,128)(2,1)}, u32[]{:S(2)}, u32[]{:S(2)}) collective-permute-start(bf16[64,2880]{1,0:T(8,128)(2,1)} %add_convert_fusion.2), channel_id=1, source_target_pairs={{0,4},{2,6},{4,8},{6,10},{8,12},{10,14},{12,0},{14,2},{1,5},{3,7},... | collective-permute-start | bytes 1105928 | tf_op jit(solution)/shard_map/sum_back/ppermute | solution.py:294
  206.6 4.5 %copy-start.15 = (bf16[128,2880]{1,0:T(8,128)(2,1)S(1)}, bf16[128,2880]{1,0:T(8,128)(2,1)}, u32[]{:S(2)}) copy-start(bf16[128,2880]{1,0:T(8,128)(2,1)} %copy-done.14) | copy-start | bytes 2211844
  206.7 4.5 %copy-start.21 = (bf16[64,2880]{1,0:T(8,128)(2,1)S(1)}, bf16[64,2880]{1,0:T(8,128)(2,1)}, u32[]{:S(2)}) copy-start(bf16[64,2880]{1,0:T(8,128)(2,1)} %copy.34) | copy-start | bytes 1105924
  210.7 12.0 %collective-permute-start.15 = (bf16[64,2880]{1,0:T(8,128)(2,1)}, bf16[64,2880]{1,0:T(8,128)(2,1)}, u32[]{:S(2)}, u32[]{:S(2)}) collective-permute-start(bf16[64,2880]{1,0:T(8,128)(2,1)} %add_convert_fusion.6), channel_id=1, source_target_pairs={{0,1},{1,0},{2,3},{3,2},{4,5},{5,4},{6,7},{7,6},{8,9},{9,8},{10,11... | collective-permute-start | bytes 1105928 | tf_op jit(solution)/shard_map/sum_back/ppermute | solution.py:297
  211.9 17.4 %collective-permute-start.8 = (bf16[64,2880]{1,0:T(8,128)(2,1)}, bf16[64,2880]{1,0:T(8,128)(2,1)}, u32[]{:S(2)}, u32[]{:S(2)}) collective-permute-start(bf16[64,2880]{1,0:T(8,128)(2,1)} %add_convert_fusion.7), channel_id=1, source_target_pairs={{0,1},{1,0},{2,3},{3,2},{4,5},{5,4},{6,7},{7,6},{8,9},{9,8},{10,11... | collective-permute-start | bytes 1105928 | tf_op jit(solution)/shard_map/sum_back/ppermute | solution.py:297
  224.7 9.8 %collective-permute-start.26 = (bf16[64,2880]{1,0:T(8,128)(2,1)}, bf16[64,2880]{1,0:T(8,128)(2,1)S(1)}, u32[]{:S(2)}, u32[]{:S(2)}) collective-permute-start(bf16[64,2880]{1,0:T(8,128)(2,1)} %add_convert_fusion.1), channel_id=1, source_target_pairs={{0,4},{2,6},{4,8},{6,10},{8,12},{10,14},{12,0},{14,2},{1,5},{3,7},... | collective-permute-start | bytes 1105928 | tf_op jit(solution)/shard_map/sum_back/ppermute | solution.py:294
  225.1 11.6 %copy-start.1 = (bf16[128,2880]{0,1:T(8,128)(2,1)S(1)}, bf16[128,2880]{0,1:T(8,128)(2,1)}, u32[]{:S(2)}) copy-start(bf16[128,2880]{0,1:T(8,128)(2,1)} %param.17) | copy-start | bytes 2211844
  (5 other events, 4.1 us)
